TPU v7x, 512 devices: a whole 4x4x16 slice. The times are simulated.
512 devices in a mesh: leaf: 32 (over y, x, core), front: 16 (over z).
Axes of the slice: x: 4, y: 4, z: 16, core: 2. Of those that a mesh axis runs over, the one named last changes fastest.
Arguments:
- leaf_pivot_block: bfloat16 [32, 2048, 256], P('leaf', 'front'), may hold values from -6 to 6
- leaf_rest_block: bfloat16 [32, 512, 256], P('leaf', 'front'), may hold values from -6 to 6
- node_pivot_block: bfloat16 [32, 2048, 256], P('leaf', 'front'), may hold values from -6 to 6
- node_rest_block: bfloat16 [32, 512, 256], P('leaf', 'front'), may hold values from -6 to 6
- leaf_vectors_pivot: bfloat16 [32, 2, 2048, 2048], P('leaf', None, 'front'), may hold values from -0.125 to 0.125
- leaf_vectors_rest: bfloat16 [32, 2, 512, 2048], P('leaf', None, 'front'), may hold values from -0.125 to 0.125
- node_vectors_pivot: bfloat16 [32, 2, 2048, 2048], P('leaf', None, 'front'), may hold values from -0.125 to 0.125
- node_vectors_rest: bfloat16 [32, 2, 512, 2048], P('leaf', None, 'front'), may hold values from -0.125 to 0.125
- stack_place: int32 [32, 1024], P('leaf'), may hold values from 0 to 2559, as said below
- parent_columns: int32 [32, 2, 512], P('leaf'), may hold values from 0 to 2047, as said below
- coupling: bfloat16 [32, 2, 2048, 512], P('leaf', None, 'front'), may hold values from -0.125 to 0.125
- pivot_inverse: bfloat16 [32, 2, 2048, 2048], P('leaf', None, 'front'), may hold values from -0.125 to 0.125
Outputs:
- solution: bfloat16 [32, 2, 2048, 256], P('leaf', None, 'front')
- remainder: bfloat16 [32, 512, 256], P('leaf', 'front')
Inputs may be any that keep to these rules, and one draw needn't show every extreme that they name: `stack_place`: each group's row holds 1024 distinct stack rows. `parent_columns`: each group's row for each slot holds 512 distinct pivot columns.
All inputs are finite; a program needn't handle non-finite values.
Results may differ from a plain program's by a relative error of at most 0.024.
Values may be sent and summed in bfloat16 or wider, within the bound.
No kernel may reach another device: no remote copies, remote signals or barrier semaphores. Data moves between devices by JAX's collectives and lax.ppermute only.
A program may use at most 64 MiB of HBM per device.

v0:
```python
import jax
import jax.numpy as jnp
from jax import lax
from jax.sharding import PartitionSpec as P

K = 2048
C = 512
LEVELS = 2


def in_one_piece(arrays, axis, dim, along):
    ends, at = ([], 0)
    for a in arrays[:-1]:
        at += a.shape[along]
        ends.append(at)
    both = jnp.concatenate(arrays, axis=along)
    return tuple(jnp.split(lax.all_gather(both, axis, axis=dim, tiled=True), ends, axis=along))


def from_behind(block, axis, distance):
    devices = range(lax.axis_size(axis))
    route = [((i - distance) % len(devices), i) for i in devices]
    return lax.ppermute(block, axis, route)


def laid_out(parts, dim):
    lengths = list(parts.shape[1:])
    lengths[dim] *= parts.shape[0]
    return jnp.moveaxis(parts, 0, dim).reshape(lengths)


def sent_to_all(shard, axis):
    copies = jnp.broadcast_to(shard, (lax.axis_size(axis), *shard.shape))
    return lax.all_to_all(copies, axis, split_axis=0, concat_axis=0, tiled=True)


def gather_directly(shard, axis, dim):
    return laid_out(sent_to_all(shard, axis), dim)


def added(first, second):
    return (first.astype(jnp.float32) + second.astype(jnp.float32)).astype(jnp.bfloat16)


def per_device(
    leaf_pivot_block,
    leaf_rest_block,
    node_pivot_block,
    node_rest_block,
    leaf_vectors_pivot,
    leaf_vectors_rest,
    node_vectors_pivot,
    node_vectors_rest,
    stack_place,
    parent_columns,
    coupling,
    pivot_inverse,
):
    subtree = 2**LEVELS
    front_index = lax.axis_index("front")
    pivot_count = leaf_vectors_pivot.shape[2]
    rest_count = leaf_vectors_rest.shape[2]

    def reflect(block_pivot, block_rest, vectors_pivot, vectors_rest):
        partial_value = jnp.einsum(
            "ik,ir->kr", vectors_pivot[1], block_pivot, preferred_element_type=jnp.float32
        )
        partial_value = partial_value + jnp.einsum(
            "ik,ir->kr", vectors_rest[1], block_rest, preferred_element_type=jnp.float32
        )
        summed = lax.psum(partial_value.astype(jnp.bfloat16), "front")
        pivots = block_pivot - jnp.dot(vectors_pivot[0], summed, preferred_element_type=jnp.float32)
        rest = block_rest - jnp.dot(vectors_rest[0], summed, preferred_element_type=jnp.float32)
        return (pivots.astype(jnp.bfloat16), rest.astype(jnp.bfloat16))

    inverse_map = (
        jnp.full((K + C,), -1, jnp.int32).at[stack_place[0]].set(jnp.arange(2 * C, dtype=jnp.int32))
    )
    pivot_rows = front_index * pivot_count + jnp.arange(pivot_count, dtype=jnp.int32)
    rest_rows = K + front_index * rest_count + jnp.arange(rest_count, dtype=jnp.int32)
    pivot_source = inverse_map[pivot_rows]
    rest_source = inverse_map[rest_rows]

    def assemble(left_part, right_part):
        left_whole, right_whole = in_one_piece((left_part, right_part), "front", 0, 1)
        joined = jnp.concatenate([left_whole, right_whole], axis=0)

        def fill_rows(own_rows, source):
            picked_rows = jnp.take(joined, jnp.maximum(source, 0), axis=0)
            return jnp.where((source >= 0)[:, None], picked_rows, own_rows)

        return (
            fill_rows(node_pivot_block[0], pivot_source),
            fill_rows(node_rest_block[0], rest_source),
        )

    def run_node(left_part, right_part):
        stack_pivots, stack_rest = assemble(left_part, right_part)
        return reflect(stack_pivots, stack_rest, node_vectors_pivot[0], node_vectors_rest[0])

    leaf_pivots, leaf_remainder = reflect(
        leaf_pivot_block[0], leaf_rest_block[0], leaf_vectors_pivot[0], leaf_vectors_rest[0]
    )
    left_part = from_behind(leaf_remainder, "leaf", 1)
    node_pivots, node_remainder = run_node(left_part, leaf_remainder)
    height = 2
    offset = 2 ** (height - 2)
    left_part = from_behind(node_remainder, "leaf", offset)
    right_part = from_behind(node_remainder, "leaf", -offset)
    node_pivots, node_remainder = run_node(left_part, right_part)
    root_part = from_behind(node_remainder, "leaf", -(subtree // 2))
    node_pivots, node_remainder = run_node(root_part, jnp.zeros_like(root_part))
    pivots_all, coupling_all = in_one_piece(
        (jnp.stack([leaf_pivots, node_pivots]), coupling[0]), "front", 1, 2
    )

    def settle(which_slot, parent, columns):
        right_side = pivots_all[which_slot].astype(jnp.float32)
        if parent is not None:
            chosen = jnp.take(parent, columns, axis=0)
            right_side = right_side - jnp.dot(
                coupling_all[which_slot], chosen, preferred_element_type=jnp.float32
            )
        result = jnp.dot(
            pivot_inverse[0, which_slot],
            right_side.astype(jnp.bfloat16),
            preferred_element_type=jnp.float32,
        )
        return result.astype(jnp.bfloat16)

    def fetch_parent(parent_part):
        return gather_directly(parent_part, "front", 0)

    node_solution = settle(1, None, None)
    for height in range(LEVELS, 0, -1):
        if height == LEVELS:
            parent_part = from_behind(node_solution, "leaf", subtree // 2)
        else:
            offset = 2 ** (height - 1)
            lower_part = from_behind(node_solution, "leaf", offset)
            higher_part = from_behind(node_solution, "leaf", -offset)
            parent_part = added(higher_part, lower_part)
        node_solution = settle(1, fetch_parent(parent_part), parent_columns[0, 1])
    from_right = from_behind(node_solution, "leaf", -1)
    parent_part = added(from_right, node_solution)
    leaf_solution = settle(0, fetch_parent(parent_part), parent_columns[0, 0])
    solution = jnp.stack([leaf_solution, node_solution])[None]
    return (solution, node_remainder[None])


def solution(mesh):
    in_specs = (
        P("leaf", "front", None),
        P("leaf", "front", None),
        P("leaf", "front", None),
        P("leaf", "front", None),
        P("leaf", None, "front", None),
        P("leaf", None, "front", None),
        P("leaf", None, "front", None),
        P("leaf", None, "front", None),
        P("leaf", None),
        P("leaf", None, None),
        P("leaf", None, "front", None),
        P("leaf", None, "front", None),
    )
    out_specs = (P("leaf", None, "front", None), P("leaf", "front", None))
    return jax.shard_map(
        per_device, mesh=mesh, in_specs=in_specs, out_specs=out_specs, check_vma=False
    )
```

profile of v0, /device:TPU:127, one launch (start us, length us, event | category | flops | bytes accessed | tf_op | source)
XLA Modules:
  0.0 993.0 jit_solution(9829018714895478358)
XLA Ops:
  7.2 1.5 fusion.46
  8.8 1.5 fusion
  10.4 4.3 scatter_custom_fusion
  14.8 1.1 gather_fusion
  16.7 125.2 %all-reduce.6.cloned.1.call-done = bf16[2048,256]{1,0:T(8,128)(2,1)} async-done(((bf16[2048,256]{1,0:T(8,128)(2,1)}), bf16[2048,256]{1,0:T(8,128)(2,1)}) %all-reduce.6.cloned.1.call-update) | async-done | bytes 1048592 | tf_op jit(solution)/shard_map/psum | solution.py:71
  141.9 1.5 fusion.32
  143.4 12.0 %collective-permute-start = (bf16[32,256]{1,0:T(8,128)(2,1)S(1)}, bf16[32,256]{1,0:T(8,128)(2,1)S(1)}, u32[]{:S(2)}, u32[]{:S(2)}) collective-permute-start(bf16[32,256]{1,0:T(8,128)(2,1)S(1)} %fusion.32), channel_id=1, source_target_pairs={{496,0},{0,16},{16,32},{32,48},{48,64},{64,80},{80,96},{96,112},{1... | collective-permute-start | bytes 49160 | tf_op jit(solution)/shard_map/ppermute | solution.py:23
  156.3 22.6 %all_gather.12 = bf16[512,512]{1,0:T(8,128)(2,1)S(1)} all-gather(bf16[32,512]{1,0:T(8,128)(2,1)S(1)} %pad_maximum_fusion.5), channel_id=1, replica_groups=mesh['leaf'=32,'front'=16] {'front'}, dimensions={0}, use_global_device_ids=true | all-gather | bytes 557056 | tf_op jit(solution)/shard_map/all_gather | solution.py:17
  181.1 1.5 fusion.9
  182.7 135.9 %all-reduce.8.cloned.1.call-done = bf16[2048,256]{0,1:T(8,128)(2,1)} async-done(((bf16[2048,256]{0,1:T(8,128)(2,1)}), bf16[2048,256]{0,1:T(8,128)(2,1)}) %all-reduce.8.cloned.1.call-update) | async-done | bytes 1048592 | tf_op jit(solution)/shard_map/psum | solution.py:71
  318.6 1.6 fusion.29
  320.2 11.9 %collective-permute-start.1 = (bf16[32,256]{1,0:T(8,128)(2,1)S(1)}, bf16[32,256]{1,0:T(8,128)(2,1)S(1)}, u32[]{:S(2)}, u32[]{:S(2)}) collective-permute-start(bf16[32,256]{1,0:T(8,128)(2,1)S(1)} %fusion.29), channel_id=1, source_target_pairs={{496,0},{0,16},{16,32},{32,48},{48,64},{64,80},{80,96},{96,112},{1... | collective-permute-start | bytes 49160 | tf_op jit(solution)/shard_map/ppermute | solution.py:23
  332.1 1.9 collective-permute-start.2
  334.1 6.4 collective-permute-done.2
  340.5 22.1 %all_gather.13 = bf16[512,512]{1,0:T(8,128)(2,1)S(1)} all-gather(bf16[32,512]{1,0:T(8,128)(2,1)S(1)} %pad_maximum_fusion.6), channel_id=1, replica_groups=mesh['leaf'=32,'front'=16] {'front'}, dimensions={0}, use_global_device_ids=true | all-gather | bytes 557056 | tf_op jit(solution)/shard_map/all_gather | solution.py:17
  364.7 1.5 fusion.8
  366.3 130.4 %all-reduce.10.cloned.1.call-done = bf16[2048,256]{0,1:T(8,128)(2,1)} async-done(((bf16[2048,256]{0,1:T(8,128)(2,1)}), bf16[2048,256]{0,1:T(8,128)(2,1)}) %all-reduce.10.cloned.1.call-update) | async-done | bytes 1048592 | tf_op jit(solution)/shard_map/psum | solution.py:71
  496.7 1.6 fusion.30
  498.3 2.5 collective-permute-start.3
  500.8 5.3 collective-permute-done.3
  506.1 22.5 %all_gather.14 = bf16[512,512]{1,0:T(8,128)(2,1)S(1)} all-gather(bf16[32,512]{1,0:T(8,128)(2,1)S(1)} %concatenate.25), channel_id=1, replica_groups=mesh['leaf'=32,'front'=16] {'front'}, dimensions={0}, use_global_device_ids=true | all-gather | bytes 557056 | tf_op jit(solution)/shard_map/all_gather | solution.py:17
  530.8 1.5 fusion.7
  532.5 1.6 fusion.24
  534.1 142.4 %all-reduce.12.cloned.1.call-done = bf16[2048,256]{0,1:T(8,128)(2,1)} async-done(((bf16[2048,256]{0,1:T(8,128)(2,1)}), bf16[2048,256]{0,1:T(8,128)(2,1)}) %all-reduce.12.cloned.1.call-update) | async-done | bytes 1048592 | tf_op jit(solution)/shard_map/psum | solution.py:71
  676.4 1.7 fusion.23
  679.1 89.4 %all-gather.2.cloned.1.call-done = bf16[2,2048,768]{2,1,0:T(8,128)(2,1)} async-done(((bf16[2,128,768]{2,1,0:T(8,128)(2,1)}), bf16[2,2048,768]{2,1,0:T(8,128)(2,1)}) %all-gather.2.cloned.1.call-update) | async-done | bytes 6291472 | tf_op jit(solution)/shard_map/all_gather | solution.py:17
  768.5 1.7 fusion.20
  770.2 2.1 collective-permute-start.4
  772.3 2.9 collective-permute-done.4
  775.4 1.2 broadcast_in_dim.86
  776.5 11.0 %all-to-all-start = ((bf16[16,128,256]{2,1,0:T(8,128)(2,1)}), bf16[16,128,256]{2,1,0:T(8,128)(2,1)S(1)}, u32[]{:S(2)}, u32[]{:S(2)}) async-start(bf16[16,128,256]{2,1,0:T(8,128)(2,1)} %broadcast_in_dim.86), calls=%async_computation | async-start | bytes 2097152 | tf_op jit(solution)/shard_map/all_to_all | solution.py:34
  787.6 46.8 %all-to-all-done = bf16[16,128,256]{2,1,0:T(8,128)(2,1)S(1)} async-done(((bf16[16,128,256]{2,1,0:T(8,128)(2,1)}), bf16[16,128,256]{2,1,0:T(8,128)(2,1)S(1)}, u32[]{:S(2)}, u32[]{:S(2)}) %all-to-all-start) | async-done | bytes 1048608 | tf_op jit(solution)/shard_map/all_to_all | solution.py:34
  834.4 1.9 gather_fusion.8
  836.3 3.3 fusion.21
  839.6 4.3 collective-permute-start.5
  844.0 5.3 collective-permute-start.6
  849.3 1.3 collective-permute-done.6
  850.8 60.4 %all_to_all.15 = bf16[16,128,256]{2,1,0:T(8,128)(2,1)S(1)} all-to-all(bf16[16,128,256]{2,1,0:T(8,128)(2,1)S(1)} %broadcast_in_dim.87), channel_id=1, replica_groups=mesh['leaf'=32,'front'=16] {'front'}, dimensions={0} | all-to-all | bytes 2097152 | tf_op jit(solution)/shard_map/all_to_all | solution.py:34
  911.2 1.9 gather_fusion.9
  913.2 3.3 fusion.19
  916.5 2.1 collective-permute-start.7
  918.5 7.0 collective-permute-done.7
  925.6 1.2 broadcast_in_dim.88
  926.8 6.7 all-to-all-start.2
  933.6 1.0 fusion.33
  934.6 45.9 %all-to-all-done.2 = bf16[16,128,256]{2,1,0:T(8,128)(2,1)S(1)} async-done(((bf16[16,128,256]{2,1,0:T(8,128)(2,1)}), bf16[16,128,256]{2,1,0:T(8,128)(2,1)S(1)}, u32[]{:S(2)}, u32[]{:S(2)}) %all-to-all-start.2) | async-done | bytes 1048608 | tf_op jit(solution)/shard_map/all_to_all | solution.py:34
  980.5 1.9 gather_fusion.10
  982.4 3.3 fusion.22
  (93 shorter events, 10.5 us)
Async XLA Ops:
  7.2 1.6 copy-start.8
  7.2 1.6 copy-start.5
  7.2 134.7 %all-reduce.6.cloned.1.call-start = ((), (), s32[]{:S(2)}) async-start(), calls=%async_computation.3 | async-start | bytes 2097152 | tf_op jit(solution)/shard_map/psum | solution.py:71
  8.8 1.6 copy-start.10
  10.3 145.2 %copy-start.9 = (bf16[1,128,256]{2,1,0:T(8,128)(2,1)S(1)}, bf16[1,128,256]{2,1,0:T(8,128)(2,1)}, u32[]{:S(2)}) copy-start(bf16[1,128,256]{2,1,0:T(8,128)(2,1)} %param.20) | copy-start | bytes 196612
  10.3 308.3 %all-reduce.8.cloned.1.call-start = ((), (), s32[]{:S(2)}) async-start(), calls=%async_computation.4 | async-start | bytes 2097152 | tf_op jit(solution)/shard_map/psum | solution.py:71
  143.4 37.2 %copy-start = (bf16[1,2,128,2048]{3,2,1,0:T(8,128)(2,1)S(1)}, bf16[1,2,128,2048]{3,2,1,0:T(8,128)(2,1)}, u32[]{:S(2)}) copy-start(bf16[1,2,128,2048]{3,2,1,0:T(8,128)(2,1)} %param.24) | copy-start | bytes 3145732
  143.4 12.9 %collective-permute-start = (bf16[32,256]{1,0:T(8,128)(2,1)S(1)}, bf16[32,256]{1,0:T(8,128)(2,1)S(1)}, u32[]{:S(2)}, u32[]{:S(2)}) collective-permute-start(bf16[32,256]{1,0:T(8,128)(2,1)S(1)} %fusion.32), channel_id=1, source_target_pairs={{496,0},{0,16},{16,32},{32,48},{48,64},{64,80},{80,96},{96,112},{1... | collective-permute-start | bytes 49160 | tf_op jit(solution)/shard_map/ppermute | solution.py:23
  179.0 2.1 copy-start.1
  179.0 2.1 copy-start.4
  182.6 314.0 %all-reduce.10.cloned.1.call-start = ((), (), s32[]{:S(2)}) async-start(), calls=%async_computation.5 | async-start | bytes 2097152 | tf_op jit(solution)/shard_map/psum | solution.py:71
  320.2 13.8 %collective-permute-start.1 = (bf16[32,256]{1,0:T(8,128)(2,1)S(1)}, bf16[32,256]{1,0:T(8,128)(2,1)S(1)}, u32[]{:S(2)}, u32[]{:S(2)}) collective-permute-start(bf16[32,256]{1,0:T(8,128)(2,1)S(1)} %fusion.29), channel_id=1, source_target_pairs={{496,0},{0,16},{16,32},{32,48},{48,64},{64,80},{80,96},{96,112},{1... | collective-permute-start | bytes 49160 | tf_op jit(solution)/shard_map/ppermute | solution.py:23
  332.1 8.4 collective-permute-start.2
  366.3 310.2 %all-reduce.12.cloned.1.call-start = ((), (), s32[]{:S(2)}) async-start(), calls=%async_computation.6 | async-start | bytes 2097152 | tf_op jit(solution)/shard_map/psum | solution.py:71
  498.3 7.8 collective-permute-start.3
  530.7 1.6 copy-start.7
  530.8 1.7 copy-start.2
  532.3 236.2 %all-gather.2.cloned.1.call-start = ((), (), s32[]{:S(2)}) async-start(), calls=%async_computation.7 | async-start | bytes 6684672 | tf_op jit(solution)/shard_map/all_gather | solution.py:17
  532.5 145.8 %copy-start.6 = (bf16[1,2,128,512]{3,2,1,0:T(8,128)(2,1)S(1)}, bf16[1,2,128,512]{3,2,1,0:T(8,128)(2,1)}, u32[]{:S(2)}) copy-start(bf16[1,2,128,512]{3,2,1,0:T(8,128)(2,1)} %param.28) | copy-start | bytes 786436
  534.1 234.4 %copy-start.12 = (bf16[1,2,128,2048]{3,2,1,0:T(8,128)(2,1)S(1)}, bf16[1,2,128,2048]{3,2,1,0:T(8,128)(2,1)}, u32[]{:S(2)}) copy-start(bf16[1,2,128,2048]{3,2,1,0:T(8,128)(2,1)} %param.29) | copy-start | bytes 3145732
  770.2 17.3 %copy-start.11 = (s32[1,2,512]{2,1,0:T(2,128)S(1)}, s32[1,2,512]{2,1,0:T(2,128)}, u32[]{:S(2)}) copy-start(s32[1,2,512]{2,1,0:T(2,128)} %param.27) | copy-start | bytes 12292
  770.2 5.0 collective-permute-start.4
  776.5 57.9 %all-to-all-start = ((bf16[16,128,256]{2,1,0:T(8,128)(2,1)}), bf16[16,128,256]{2,1,0:T(8,128)(2,1)S(1)}, u32[]{:S(2)}, u32[]{:S(2)}) async-start(bf16[16,128,256]{2,1,0:T(8,128)(2,1)} %broadcast_in_dim.86), calls=%async_computation | async-start | bytes 2097152 | tf_op jit(solution)/shard_map/all_to_all | solution.py:34
  839.6 9.7 collective-permute-start.5
  844.0 6.6 collective-permute-start.6
  916.4 17.1 %copy-start.3 = (bf16[2048,256]{0,1:T(8,128)(2,1)S(1)}, bf16[2048,256]{0,1:T(8,128)(2,1)}, u32[]{:S(2)}) copy-start(bf16[2048,256]{0,1:T(8,128)(2,1)} %all-reduce.12.cloned.1.call-done) | copy-start | bytes 3145732
  916.5 9.0 collective-permute-start.7
  926.8 53.7 %all-to-all-start.2 = ((bf16[16,128,256]{2,1,0:T(8,128)(2,1)}), bf16[16,128,256]{2,1,0:T(8,128)(2,1)S(1)}, u32[]{:S(2)}, u32[]{:S(2)}) async-start(bf16[16,128,256]{2,1,0:T(8,128)(2,1)} %broadcast_in_dim.88), calls=%async_computation.2 | async-start | bytes 2097152 | tf_op jit(solution)/shard_map/all_to_all | solution.py:34
Sparse Core Ops, SparseCore 0:
  10.4 131.4 all-reduce.5
  182.8 135.7 all-reduce.7
  366.4 130.2 all-reduce.9
  532.4 143.9 all-reduce.11
  679.2 89.2 all-gather.1
where the time goes:
time: 994 us; the launch traced here: 993 us
  waiting for transfers between devices  740 us (74%)
  blocking collectives  128 us (13%)
  starting transfers between devices  60 us (6%)
  matrix products  29.4 us (3%)
  local copies, waits for them, and re-layouts  20.8 us (2%)
  between operations  14.4 us (1%)
    psum x4, waiting for transfers between devices, reflect(): summed = lax.psum(partial_value.astype(jnp.bfloat16), 'front')  534 us
    all_to_all x2, waiting for transfers between devices, sent_to_all(): return lax.all_to_all(copies, axis, split_axis=0, concat_axis=0, tiled=True)  92.7 us
    all_gather x1, waiting for transfers between devices, in_one_piece(): lax.all_gather(both, axis, axis=dim, tiled=True)  89.4 us
    all_gather x3, blocking collectives, in_one_piece(): lax.all_gather(both, axis, axis=dim, tiled=True)  67.2 us
    all_to_all x1, blocking collectives, sent_to_all(): return lax.all_to_all(copies, axis, split_axis=0, concat_axis=0, tiled=True)  60.4 us
    ppermute x8, starting transfers between devices, from_behind(): return lax.ppermute(block, axis, route)  42.1 us
    ppermute x8, waiting for transfers between devices, from_behind(): return lax.ppermute(block, axis, route)  23.6 us
  transfers between devices with their start and end apart: 15, of which 13 were waited for; matrix products, arithmetic and copies ran while one was open for 1% of the time, Pallas kernels for 0%

commit v1 on v0

--- a/solution.py
+++ b/solution.py
@@ -68,7 +68,7 @@
         partial_value = partial_value + jnp.einsum(
             "ik,ir->kr", vectors_rest[1], block_rest, preferred_element_type=jnp.float32
         )
-        summed = lax.psum(partial_value.astype(jnp.bfloat16), "front")
+        summed = jnp.sum(lax.all_gather(partial_value.astype(jnp.bfloat16), "front"), axis=0)
         pivots = block_pivot - jnp.dot(vectors_pivot[0], summed, preferred_element_type=jnp.float32)
         rest = block_rest - jnp.dot(vectors_rest[0], summed, preferred_element_type=jnp.float32)
         return (pivots.astype(jnp.bfloat16), rest.astype(jnp.bfloat16))

time: 994 us -> 1290 us (1.30)
  the two profiles are of different devices: /device:TPU:127 before, /device:TPU:13 now
where the time goes in v1:
time: 1290 us
  waiting for transfers between devices  969 us (75%)
  blocking collectives  131 us (10%)
  local copies, waits for them, and re-layouts  68.6 us (5%)
  starting transfers between devices  43 us (3%)
  other arithmetic  34.4 us (3%)
  matrix products  25.7 us (2%)
  between operations  14.6 us (1%)
    all_gather x4, waiting for transfers between devices, reflect(): lax.all_gather(partial_value.astype(jnp.bfloat16), 'front')  779 us
    all_to_all x2, waiting for transfers between devices, sent_to_all(): return lax.all_to_all(copies, axis, split_axis=0, concat_axis=0, tiled=True)  93.9 us
    all_gather x1, waiting for transfers between devices, in_one_piece(): lax.all_gather(both, axis, axis=dim, tiled=True)  82.3 us
    all_gather x3, blocking collectives, in_one_piece(): lax.all_gather(both, axis, axis=dim, tiled=True)  72.2 us
    all_to_all x1, blocking collectives, sent_to_all(): return lax.all_to_all(copies, axis, split_axis=0, concat_axis=0, tiled=True)  59.2 us
    unnamed x48, local copies, waits for them, and re-layouts  48.4 us
    reduce_sum x4, other arithmetic, reflect(): jnp.sum(lax.all_gather(partial_value.astype(jnp.bfloat16), 'front'), axis=0)  33.3 us
    ppermute x8, starting transfers between devices, from_behind(): return lax.ppermute(block, axis, route)  26.5 us
  transfers between devices with their start and end apart: 15, of which 13 were waited for; matrix products, arithmetic and copies ran while one was open for 1% of the time, Pallas kernels for 0%

profile of v1, /device:TPU:13, one launch (start us, length us, event | category | flops | bytes accessed | tf_op | source)
XLA Modules:
  0.0 1286.5 jit_solution(15286955092665730789)
XLA Ops:
  7.2 1.5 fusion.46
  8.8 1.5 fusion
  10.4 4.3 scatter_custom_fusion
  16.7 188.3 %all-gather.12.cloned.1.call-done = bf16[32768,256]{1,0:T(8,128)(2,1)} async-done(((bf16[2048,256]{1,0:T(8,128)(2,1)}), bf16[32768,256]{1,0:T(8,128)(2,1)}) %all-gather.12.cloned.1.call-update) | async-done | bytes 16777232 | tf_op jit(solution)/shard_map/all_gather | solution.py:71
  205.0 8.9 reduce_sum.48
  214.2 3.5 collective-permute-start
  218.5 23.9 %all_gather.38 = bf16[512,512]{1,0:T(8,128)(2,1)S(1)} all-gather(bf16[32,512]{1,0:T(8,128)(2,1)S(1)} %pad_maximum_fusion.5), channel_id=1, replica_groups=mesh['leaf'=32,'front'=16] {'front'}, dimensions={0}, use_global_device_ids=true | all-gather | bytes 557056 | tf_op jit(solution)/shard_map/all_gather | solution.py:17
  244.6 1.5 fusion.9
  246.1 196.5 %all-gather.14.cloned.1.call-done = bf16[32768,256]{0,1:T(8,128)(2,1)} async-done(((bf16[2048,256]{0,1:T(8,128)(2,1)}), bf16[32768,256]{0,1:T(8,128)(2,1)}) %all-gather.14.cloned.1.call-update) | async-done | bytes 16777232 | tf_op jit(solution)/shard_map/all_gather | solution.py:71
  442.7 15.1 %copy.44 = bf16[32,8,16,2048]{3,2,1,0:T(8,128)(2,1)S(1)} copy(bf16[32,8,16,2048]{3,1,2,0:T(8,128)(2,1)} %bitcast.221) | data formatting | bytes 33554432
  457.8 8.1 bitcast_reduce_fusion.2
  466.3 2.6 collective-permute-start.2
  468.9 3.0 collective-permute-start.1
  472.8 24.2 %all_gather.41 = bf16[512,512]{1,0:T(8,128)(2,1)S(1)} all-gather(bf16[32,512]{1,0:T(8,128)(2,1)S(1)} %pad_maximum_fusion.6), channel_id=1, replica_groups=mesh['leaf'=32,'front'=16] {'front'}, dimensions={0}, use_global_device_ids=true | all-gather | bytes 557056 | tf_op jit(solution)/shard_map/all_gather | solution.py:17
  499.1 1.5 fusion.8
  500.8 198.7 %all-gather.16.cloned.1.call-done = bf16[32768,256]{0,1:T(8,128)(2,1)} async-done(((bf16[2048,256]{0,1:T(8,128)(2,1)}), bf16[32768,256]{0,1:T(8,128)(2,1)}) %all-gather.16.cloned.1.call-update) | async-done | bytes 16777232 | tf_op jit(solution)/shard_map/all_gather | solution.py:71
  699.5 15.1 %copy.45 = bf16[32,8,16,2048]{3,2,1,0:T(8,128)(2,1)S(1)} copy(bf16[32,8,16,2048]{3,1,2,0:T(8,128)(2,1)} %bitcast.222) | data formatting | bytes 33554432
  714.6 8.1 bitcast_reduce_fusion.1
  723.2 2.2 collective-permute-start.3
  725.4 2.3 collective-permute-done.3
  727.7 24.1 %all_gather.44 = bf16[512,512]{1,0:T(8,128)(2,1)S(1)} all-gather(bf16[32,512]{1,0:T(8,128)(2,1)S(1)} %concatenate.25), channel_id=1, replica_groups=mesh['leaf'=32,'front'=16] {'front'}, dimensions={0}, use_global_device_ids=true | all-gather | bytes 557056 | tf_op jit(solution)/shard_map/all_gather | solution.py:17
  751.9 1.2 gather_fusion.7
  754.8 2.2 fusion.7
  757.1 1.6 copy.34
  758.7 2.0 fusion.24
  760.6 195.8 %all-gather.18.cloned.1.call-done = bf16[32768,256]{0,1:T(8,128)(2,1)} async-done(((bf16[2048,256]{0,1:T(8,128)(2,1)}), bf16[32768,256]{0,1:T(8,128)(2,1)}) %all-gather.18.cloned.1.call-update) | async-done | bytes 16777232 | tf_op jit(solution)/shard_map/all_gather | solution.py:71
  956.4 15.1 %copy.46 = bf16[32,8,16,2048]{3,2,1,0:T(8,128)(2,1)S(1)} copy(bf16[32,8,16,2048]{3,1,2,0:T(8,128)(2,1)} %bitcast.220) | data formatting | bytes 33554432
  971.5 8.1 bitcast_reduce_fusion
  981.5 82.3 %all-gather.10.cloned.1.call-done = bf16[2,2048,768]{2,1,0:T(8,128)(2,1)} async-done(((bf16[2,128,768]{2,1,0:T(8,128)(2,1)}), bf16[2,2048,768]{2,1,0:T(8,128)(2,1)}) %all-gather.10.cloned.1.call-update) | async-done | bytes 6291472 | tf_op jit(solution)/shard_map/all_gather | solution.py:17
  1063.8 1.9 fusion.20
  1065.6 2.8 collective-permute-start.4
  1068.4 2.2 collective-permute-done.4
  1071.8 9.2 all-to-all-start
  1081.2 44.4 %all-to-all-done = bf16[16,128,256]{2,1,0:T(8,128)(2,1)S(1)} async-done(((bf16[16,128,256]{2,1,0:T(8,128)(2,1)}), bf16[16,128,256]{2,1,0:T(8,128)(2,1)S(1)}, u32[]{:S(2)}, u32[]{:S(2)}) %all-to-all-start) | async-done | bytes 1048608 | tf_op jit(solution)/shard_map/all_to_all | solution.py:34
  1125.5 1.9 gather_fusion.8
  1127.5 3.3 fusion.21
  1130.8 8.6 collective-permute-start.6
  1139.3 1.9 collective-permute-start.5
  1141.3 3.6 collective-permute-done.5
  1145.2 59.2 %all_to_all.15 = bf16[16,128,256]{2,1,0:T(8,128)(2,1)S(1)} all-to-all(bf16[16,128,256]{2,1,0:T(8,128)(2,1)S(1)} %broadcast_in_dim.87), channel_id=1, replica_groups=mesh['leaf'=32,'front'=16] {'front'}, dimensions={0} | all-to-all | bytes 2097152 | tf_op jit(solution)/shard_map/all_to_all | solution.py:34
  1204.3 1.9 gather_fusion.9
  1206.3 3.3 fusion.19
  1209.6 1.9 collective-permute-start.7
  1211.5 3.7 collective-permute-done.7
  1216.4 6.9 all-to-all-start.2
  1224.4 49.5 %all-to-all-done.2 = bf16[16,128,256]{2,1,0:T(8,128)(2,1)S(1)} async-done(((bf16[16,128,256]{2,1,0:T(8,128)(2,1)}), bf16[16,128,256]{2,1,0:T(8,128)(2,1)S(1)}, u32[]{:S(2)}, u32[]{:S(2)}) %all-to-all-start.2) | async-done | bytes 1048608 | tf_op jit(solution)/shard_map/all_to_all | solution.py:34
  1273.9 1.9 gather_fusion.10
  1275.9 3.3 fusion.22
  (116 shorter events, 17.4 us)
Async XLA Ops:
  7.2 1.6 copy-start.3
  7.2 1.6 copy-start.8
  7.2 197.8 %all-gather.12.cloned.1.call-start = ((), (), s32[]{:S(2)}) async-start(), calls=%async_computation.4 | async-start | bytes 17825792 | tf_op jit(solution)/shard_map/all_gather | solution.py:71
  8.8 1.5 copy-start.19
  10.3 432.4 %all-gather.14.cloned.1.call-start = ((), (), s32[]{:S(2)}) async-start(), calls=%async_computation.5 | async-start | bytes 17825792 | tf_op jit(solution)/shard_map/all_gather | solution.py:71
  16.7 706.1 %copy-start.11 = (pred[32]{0:T(512)(128)(4,1)}, pred[32]{0:T(512)(128)(4,1)S(1)}, u32[]{:S(2)}) copy-start(pred[32]{0:T(512)(128)(4,1)S(1)} %get-tuple-element.19) | copy-start | bytes 100
  16.7 706.1 %copy-start.13 = (pred[32]{0:T(512)(128)(4,1)}, pred[32]{0:T(512)(128)(4,1)S(1)}, u32[]{:S(2)}) copy-start(pred[32]{0:T(512)(128)(4,1)S(1)} %get-tuple-element.20) | copy-start | bytes 100
  16.7 737.4 %copy-start.15 = (pred[128]{0:T(512)(128)(4,1)}, pred[128]{0:T(512)(128)(4,1)S(1)}, u32[]{:S(2)}) copy-start(pred[128]{0:T(512)(128)(4,1)S(1)} %get-tuple-element.21) | copy-start | bytes 388
  16.7 737.4 %copy-start.17 = (pred[128]{0:T(512)(128)(4,1)}, pred[128]{0:T(512)(128)(4,1)S(1)}, u32[]{:S(2)}) copy-start(pred[128]{0:T(512)(128)(4,1)S(1)} %get-tuple-element.22) | copy-start | bytes 388
  205.0 12.7 copy-start.9
  214.2 30.0 %copy-start = (bf16[1,2,128,2048]{3,2,1,0:T(8,128)(2,1)S(1)}, bf16[1,2,128,2048]{3,2,1,0:T(8,128)(2,1)}, u32[]{:S(2)}) copy-start(bf16[1,2,128,2048]{3,2,1,0:T(8,128)(2,1)} %param.24) | copy-start | bytes 3145732
  214.2 4.3 collective-permute-start
  242.4 2.1 copy-start.1
  242.5 2.1 copy-start.2
  246.1 453.4 %all-gather.16.cloned.1.call-start = ((), (), s32[]{:S(2)}) async-start(), calls=%async_computation.6 | async-start | bytes 17825792 | tf_op jit(solution)/shard_map/all_gather | solution.py:71
  466.3 5.6 collective-permute-start.2
  468.9 3.8 collective-permute-start.1
  500.6 455.8 %all-gather.18.cloned.1.call-start = ((), (), s32[]{:S(2)}) async-start(), calls=%async_computation.7 | async-start | bytes 17825792 | tf_op jit(solution)/shard_map/all_gather | solution.py:71
  723.2 4.5 collective-permute-start.3
  754.1 0.7 copy-start.6
  754.8 3.9 copy-start.5
  757.1 306.7 %all-gather.10.cloned.1.call-start = ((), (), s32[]{:S(2)}) async-start(), calls=%async_computation.3 | async-start | bytes 6684672 | tf_op jit(solution)/shard_map/all_gather | solution.py:17
  971.5 8.2 copy-start.16
  971.5 8.2 copy-start.18
  971.5 8.6 copy-start.10
  979.7 1.0 copy-start.4
  1065.6 15.5 %copy-start.20 = (s32[1,2,512]{2,1,0:T(2,128)S(1)}, s32[1,2,512]{2,1,0:T(2,128)}, u32[]{:S(2)}) copy-start(s32[1,2,512]{2,1,0:T(2,128)} %param.27) | copy-start | bytes 12292
  1065.6 5.0 collective-permute-start.4
  1071.8 53.7 %all-to-all-start = ((bf16[16,128,256]{2,1,0:T(8,128)(2,1)}), bf16[16,128,256]{2,1,0:T(8,128)(2,1)S(1)}, u32[]{:S(2)}, u32[]{:S(2)}) async-start(bf16[16,128,256]{2,1,0:T(8,128)(2,1)} %broadcast_in_dim.86), calls=%async_computation | async-start | bytes 2097152 | tf_op jit(solution)/shard_map/all_to_all | solution.py:34
  1130.8 10.5 collective-permute-start.6
  1139.3 5.6 collective-permute-start.5
  1209.6 13.8 %copy-start.7 = (bf16[32,256]{1,0:T(8,128)(2,1)S(1)}, bf16[32,256]{1,0:T(8,128)(2,1)}, u32[]{:S(2)}) copy-start(bf16[32,256]{1,0:T(8,128)(2,1)} %gather_fusion.7) | copy-start | bytes 49156
  1209.6 13.8 %copy-start.12 = (pred[32]{0:T(512)(128)(4,1)S(1)}, pred[32]{0:T(512)(128)(4,1)}, u32[]{:S(2)}) copy-start(pred[32]{0:T(512)(128)(4,1)} %copy-done.11) | copy-start | bytes 100
  1209.6 13.8 %copy-start.14 = (pred[32]{0:T(512)(128)(4,1)S(1)}, pred[32]{0:T(512)(128)(4,1)}, u32[]{:S(2)}) copy-start(pred[32]{0:T(512)(128)(4,1)} %copy-done.13) | copy-start | bytes 100
  1209.6 5.6 collective-permute-start.7
  1216.4 57.5 %all-to-all-start.2 = ((bf16[16,128,256]{2,1,0:T(8,128)(2,1)}), bf16[16,128,256]{2,1,0:T(8,128)(2,1)S(1)}, u32[]{:S(2)}, u32[]{:S(2)}) async-start(bf16[16,128,256]{2,1,0:T(8,128)(2,1)} %broadcast_in_dim.88), calls=%async_computation.2 | async-start | bytes 2097152 | tf_op jit(solution)/shard_map/all_to_all | solution.py:34
Sparse Core Ops, SparseCore 0:
  10.4 194.5 all-gather.11
  246.2 196.4 all-gather.13
  500.7 198.7 all-gather.15
  757.2 199.2 all-gather.17
  981.6 82.0 all-gather.9
